TPU v7x, 32 devices: a whole 2x2x4 slice. The times are simulated.
32 devices in a mesh: ctx: 4 (over y, x), dp: 8 (over z, core).
Axes of the slice: x: 2, y: 2, z: 4, core: 2. Of those that a mesh axis runs over, the one named last changes fastest.
Arguments:
- queries: bfloat16 [8, 512, 2048], P('dp', 'ctx'), may hold values from -8 to 8
- key_rows: bfloat16 [8, 512, 256], P('dp', 'ctx'), may hold values from -8 to 8
- value_rows: bfloat16 [8, 512, 256], P('dp', 'ctx'), may hold values from -6 to 6
- stream: bfloat16 [8, 512, 2048], P('dp', 'ctx'), may hold values from -6 to 6
- norm_gain: float32 [2048], replicated, may hold values from 0.1 to 1.9
- expert_ids: int32 [8, 512, 8], P('dp', 'ctx'), may hold values from 0 to 127, all different within a row; in each aligned block of 128 rows (0 to 127, 128 to 255, ..., all dimensions but the last counted through in order) at most 12 rows name the same one
- gate_values: float32 [8, 512, 8], P('dp', 'ctx'), may hold values from 0.1 to 1
- w_gate: bfloat16 [8, 2048, 384], P('dp', 'ctx'), may hold values from -0.125 to 0.125
- w_up: bfloat16 [8, 2048, 384], P('dp', 'ctx'), may hold values from -0.125 to 0.125
- w_down: bfloat16 [8, 384, 2048], P('dp', None, 'ctx'), may hold values from -0.3125 to 0.3125
Outputs:
- attended: bfloat16 [8, 512, 2048], P('dp', 'ctx')
- expert_out: bfloat16 [8, 512, 2048], P('dp', 'ctx')
Inputs may be any that keep to these rules, and one draw needn't show every extreme that they name: `expert_ids`: among the rows of one device, no expert is chosen by more than 12 rows; some expert reaches 12.
All inputs are finite; a program needn't handle non-finite values.
Results may differ from a plain program's by a relative error of at most 0.012.
Values may be sent and summed in bfloat16 or wider, within the bound.
A program may use at most 64 MiB of HBM per device.

v0:
```python
import functools
import math

import jax
import jax.numpy as jnp
from jax import lax
from jax.experimental import pallas as pl
from jax.experimental.pallas import tpu as pltpu
from jax.sharding import PartitionSpec as P

HD = 128
CAP = 12
TILE = 16
LANES = 128
MESH = pl.DeviceIdType.MESH
hidden_score = -1e30


def message_form(col):
    chunks = col // LANES
    if chunks * CAP % TILE == 0:
        return CAP, chunks
    return TILE, 1


def fused(
    n_ctx, n_dp, split,
    q_hbm, k_hbm, v_hbm, s_hbm, gain_hbm, ids_hbm, gv_hbm, wg_hbm, wu_hbm, wd_hbm,
    att_ref, out_ref,
    q_ref, s_ref, normed_ref, gain_ref, ids_ref, gv_ref, wgu, wd_ref,
    outgoing, arrived, kbuf, vbuf, rs_out, rs_in, own, hid, answers, ret,
    w_back, probs_ref, mass_ref, sort, unsort,
    k_send, k_recv, v_send, v_recv, a_send, a_recv, p_send, p_recv, h_send, h_recv,
    r_send, r_recv, load_sem,
):
    my_c = lax.axis_index("ctx")
    my_d = lax.axis_index("dp")
    me = my_c * n_dp + my_d
    total = n_ctx * n_dp
    tokens, width = s_ref.shape
    col = width // n_ctx
    slot, chunks = message_form(col)
    message = slot * chunks
    wide = col // chunks
    rows_all = n_dp * slot
    lines = n_dp * message
    units = wd_ref.shape[0]
    heads = q_ref.shape[1] // HD
    kv_heads = kbuf.shape[2] // HD
    group = heads // kv_heads

    pairs = (
        (ids_hbm.at[0], ids_ref),
        (gv_hbm.at[0], gv_ref),
        (s_hbm.at[0], s_ref),
        (gain_hbm, gain_ref),
        (wg_hbm.at[0], wgu.at[:, pl.ds(0, units)]),
        (wu_hbm.at[0], wgu.at[:, pl.ds(units, units)]),
        (k_hbm.at[0], kbuf.at[my_c]),
        (v_hbm.at[0], vbuf.at[my_c]),
        (q_hbm.at[0], q_ref),
        (wd_hbm.at[0], wd_ref),
    )
    loads = [pltpu.make_async_copy(a, b, load_sem.at[i]) for i, (a, b) in enumerate(pairs)]
    for load in loads:
        load.start()

    barrier = pltpu.get_barrier_semaphore()

    def greet(i, carry):
        peer = lax.rem(me + i, total)
        pl.semaphore_signal(
            barrier, inc=1, device_id=(peer // n_dp, lax.rem(peer, n_dp)), device_id_type=MESH
        )
        return carry

    lax.fori_loop(1, total, greet, 0)

    def parts_of(line):
        rest = lax.rem(line, message)
        return lax.div(line, message), lax.div(rest, slot), lax.rem(rest, slot)

    expert, chunk, place_rank = parts_of(lax.broadcasted_iota(jnp.int32, (lines, 1), 0))
    _, chunk_lane, rank_lane = parts_of(lax.broadcasted_iota(jnp.int32, (1, lines), 1))
    expert_lane = lax.div(lax.broadcasted_iota(jnp.int32, (1, lines), 1), message)
    loads[0].wait()
    loads[1].wait()
    hot = jnp.zeros((lines, tokens), jnp.float32)
    weight = jnp.zeros((lines, tokens), jnp.float32)
    for t in range(ids_ref.shape[0]):
        hit = ids_ref[t : t + 1, :] == expert
        hot = jnp.where(hit, 1.0, hot)
        weight = jnp.where(hit, gv_ref[t : t + 1, :], weight)
    rows_i = lax.broadcasted_iota(jnp.int32, (tokens, tokens), 0)
    cols_i = lax.broadcasted_iota(jnp.int32, (tokens, tokens), 1)
    before = jnp.where(rows_i < cols_i, 1.0, 0.0).astype(jnp.bfloat16)
    rank = jnp.dot(hot.astype(jnp.bfloat16), before, preferred_element_type=jnp.float32)
    place = jnp.where(rank == place_rank.astype(jnp.float32), hot, 0.0)
    select = jnp.concatenate(
        [jnp.where(chunk == j, place, 0.0).astype(jnp.bfloat16) for j in range(chunks)], axis=1
    )

    pl.semaphore_wait(barrier, total - 1)

    def ctx_copy(src, dst, send, recv, c):
        return pltpu.make_async_remote_copy(
            src_ref=src, dst_ref=dst, send_sem=send, recv_sem=recv,
            device_id=(c, my_d), device_id_type=MESH,
        )

    others = [lax.rem(my_c + i, n_ctx) for i in range(1, n_ctx)]
    my_rows = pl.ds(pl.multiple_of(my_d * message, message), message)

    def scatter(src, dst, send, recv, c, first):
        def one(i, carry):
            d = lax.rem(my_d + i, n_dp)
            pltpu.make_async_remote_copy(
                src_ref=src.at[c, pl.ds(pl.multiple_of(d * message, message), message)],
                dst_ref=dst.at[my_c, my_rows],
                send_sem=send.at[c],
                recv_sem=recv.at[my_c],
                device_id=(c, d),
                device_id_type=MESH,
            ).start()
            return carry

        lax.fori_loop(first, n_dp, one, 0)

    def group_of(buf, send, recv, c, rows):
        part = buf.at[c, pl.ds(0, rows)]
        return pltpu.make_async_remote_copy(
            src_ref=part, dst_ref=part, send_sem=send.at[c], recv_sem=recv.at[c],
            device_id=(c, lax.rem(my_d + 1, n_dp)), device_id_type=MESH,
        )

    for c in others:
        ctx_copy(k_hbm.at[0], kbuf.at[my_c], k_send.at[c], k_recv.at[my_c], c).start()

    loads[2].wait()
    loads[3].wait()
    x = s_ref[...].astype(jnp.float32)
    normed = (
        x * lax.rsqrt(jnp.mean(x * x, axis=-1, keepdims=True) + 1e-06) * gain_ref[...]
    ).astype(jnp.bfloat16)
    normed_ref[...] = normed
    for i, c in enumerate(others + [my_c]):
        stacked = jnp.concatenate(
            [
                normed_ref[:, pl.ds(pl.multiple_of(c * col + j * wide, wide), wide)]
                for j in range(chunks)
            ],
            axis=0,
        )
        outgoing[c] = jnp.dot(select, stacked, preferred_element_type=jnp.float32).astype(
            jnp.bfloat16
        )
        scatter(outgoing, arrived, a_send, a_recv, c, 1 if i == n_ctx - 1 else 0)
    arrived[my_c, my_rows] = outgoing[my_c, my_rows]

    if chunks > 1:
        goes = chunk * rows_all + expert * slot + place_rank
        goes_lane = chunk_lane * rows_all + expert_lane * slot + rank_lane
        square = (lines, lines)
        unsort[...] = jnp.where(
            lax.broadcasted_iota(jnp.int32, square, 1) == goes, 1.0, 0.0
        ).astype(jnp.bfloat16)
        sort[...] = jnp.where(
            lax.broadcasted_iota(jnp.int32, square, 0) == goes_lane, 1.0, 0.0
        ).astype(jnp.bfloat16)

    back = (place * weight).T
    for j in range(chunks):
        w_back[j * tokens : (j + 1) * tokens] = jnp.where(chunk_lane == j, back, 0.0).astype(
            jnp.bfloat16
        )

    keys = n_ctx * tokens
    scale = 1.0 / math.sqrt(HD)

    def kv_lanes(pair):
        return pl.ds(pl.multiple_of((2 * pair // group) * HD, HD), HD)

    def head_lanes(head):
        return pl.ds(pl.multiple_of(head * HD, HD), HD)

    def weigh(first, last):
        def one(pair, carry):
            two = jnp.concatenate([q_ref[:, head_lanes(2 * pair + i)] for i in range(2)], axis=0)
            scores = lax.dot_general(
                two, kbuf[:, :, kv_lanes(pair)].reshape(keys, HD), (((1,), (1,)), ((), ())),
                preferred_element_type=jnp.float32,
            ) * scale
            q_pos = lax.broadcasted_iota(jnp.int32, (2 * tokens, keys), 0)
            q_pos = my_c * tokens + jnp.where(q_pos < tokens, q_pos, q_pos - tokens)
            k_pos = lax.broadcasted_iota(jnp.int32, (2 * tokens, keys), 1)
            scores = jnp.where(k_pos <= q_pos, scores, hidden_score)
            probs = jnp.exp(scores - jnp.max(scores, axis=-1, keepdims=True))
            mass = jnp.sum(probs, axis=-1, keepdims=True)
            probs_ref[pair] = probs.astype(jnp.bfloat16)
            mass_ref[pair] = jnp.broadcast_to(mass, (2 * tokens, HD))
            return carry

        lax.fori_loop(first, last, one, 0)

    def mix_values():
        def one(pair, carry):
            mixed = jnp.dot(
                probs_ref[pair], vbuf[:, :, kv_lanes(pair)].reshape(keys, HD),
                preferred_element_type=jnp.float32,
            )
            done = (mixed / mass_ref[pair]).astype(jnp.bfloat16)
            for i in range(2):
                att_ref[0, :, head_lanes(2 * pair + i)] = done[i * tokens : (i + 1) * tokens]
            return carry

        lax.fori_loop(0, heads // 2, one, 0)

    marks = [heads // 2 * part // 8 for part in split]
    loads[6].wait()
    loads[8].wait()
    for c in others:
        ctx_copy(k_hbm.at[0], kbuf.at[c], k_send.at[c], k_recv.at[c], c).wait_recv()
    weigh(0, marks[0])

    def partial(c):
        block = arrived[c]
        if chunks > 1:
            block = jnp.dot(sort[...], block, preferred_element_type=jnp.float32).astype(
                jnp.bfloat16
            )
            block = jnp.concatenate(
                [block[j * rows_all : (j + 1) * rows_all] for j in range(chunks)], axis=1
            )
        return jnp.dot(block, wgu[...], preferred_element_type=jnp.float32)

    loads[4].wait()
    loads[5].wait()
    for c in others:
        group_of(arrived, a_send, a_recv, c, lines).wait_recv()
        rs_out[c] = partial(c).astype(jnp.bfloat16)
        ctx_copy(rs_out.at[c], rs_in.at[my_c], p_send.at[c], p_recv.at[my_c], c).start()
    group_of(arrived, a_send, a_recv, my_c, lines - message).wait_recv()
    own[...] = partial(my_c)
    loads[7].wait()
    loads[9].wait()
    weigh(marks[0], marks[1])
    for c in others:
        ctx_copy(rs_out.at[c], rs_in.at[c], p_send.at[c], p_recv.at[c], c).wait_recv()
    sums = own[...]
    for c in others:
        sums = sums + rs_in[c].astype(jnp.float32)
    gate = sums[:, :units]
    hid[my_c] = (gate / (1.0 + jnp.exp(-gate)) * sums[:, units:]).astype(jnp.bfloat16)
    for c in others:
        ctx_copy(hid.at[my_c], hid.at[my_c], h_send.at[c], h_recv.at[my_c], c).start()
    for c in others:
        ctx_copy(v_hbm.at[0], vbuf.at[my_c], v_send.at[c], v_recv.at[my_c], c).start()

    def answer(c):
        block = jnp.dot(hid[c], wd_ref[...], preferred_element_type=jnp.float32).astype(
            jnp.bfloat16
        )
        if chunks > 1:
            block = jnp.concatenate(
                [block[:, j * wide : (j + 1) * wide] for j in range(chunks)], axis=0
            )
            block = jnp.dot(unsort[...], block, preferred_element_type=jnp.float32).astype(
                jnp.bfloat16
            )
        answers[c] = block

    answer(my_c)
    scatter(answers, ret, r_send, r_recv, my_c, 1)
    ret[my_c, my_rows] = answers[my_c, my_rows]
    weigh(marks[1], heads // 2)
    for c in others:
        ctx_copy(hid.at[my_c], hid.at[c], h_send.at[c], h_recv.at[c], c).wait_recv()
        answer(c)
        scatter(answers, ret, r_send, r_recv, c, 0)
    for c in others:
        ctx_copy(v_hbm.at[0], vbuf.at[c], v_send.at[c], v_recv.at[c], c).wait_recv()
    mix_values()

    def combine(c):
        part = ret[c]
        mixed = jnp.dot(w_back[...], part, preferred_element_type=jnp.float32)
        mixed = jnp.concatenate(
            [mixed[j * tokens : (j + 1) * tokens] for j in range(chunks)], axis=1
        )
        out_ref[0, :, pl.ds(pl.multiple_of(c * col, col), col)] = mixed.astype(jnp.bfloat16)

    group_of(ret, r_send, r_recv, my_c, lines - message).wait_recv()
    combine(my_c)
    for c in others:
        group_of(ret, r_send, r_recv, c, lines).wait_recv()
        combine(c)

    group_of(outgoing, a_send, a_recv, my_c, lines - message).wait_send()
    group_of(answers, r_send, r_recv, my_c, lines - message).wait_send()
    for c in others:
        ctx_copy(k_hbm.at[0], kbuf.at[c], k_send.at[c], k_recv.at[c], c).wait_send()
        ctx_copy(v_hbm.at[0], vbuf.at[c], v_send.at[c], v_recv.at[c], c).wait_send()
        group_of(outgoing, a_send, a_recv, c, lines).wait_send()
        ctx_copy(rs_out.at[c], rs_in.at[c], p_send.at[c], p_recv.at[c], c).wait_send()
        ctx_copy(hid.at[my_c], hid.at[c], h_send.at[c], h_recv.at[c], c).wait_send()
        group_of(answers, r_send, r_recv, c, lines).wait_send()


def shards(
    n_ctx, n_dp, queries, key_rows, value_rows, stream, norm_gain, expert_ids, gate_values,
    w_gate, w_up, w_down,
):
    tokens, width = stream.shape[1:]
    top = expert_ids.shape[2]
    kv = key_rows.shape[2]
    units = w_gate.shape[2]
    col = width // n_ctx
    slot, chunks = message_form(col)
    rows = n_dp * slot
    lines = rows * chunks
    wide = col // chunks
    heads = queries.shape[2] // HD
    order = lines if chunks > 1 else TILE
    bf16, f32 = jnp.bfloat16, jnp.float32
    scratch = [
        ((tokens, queries.shape[2]), bf16),
        ((tokens, width), bf16),
        ((tokens, width), bf16),
        ((1, width), f32),
        ((top, tokens), jnp.int32),
        ((top, tokens), f32),
        ((col, 2 * units), bf16),
        ((units, col), bf16),
        ((n_ctx, lines, wide), bf16),
        ((n_ctx, lines, wide), bf16),
        ((n_ctx, tokens, kv), bf16),
        ((n_ctx, tokens, kv), bf16),
        ((n_ctx, rows, 2 * units), bf16),
        ((n_ctx, rows, 2 * units), bf16),
        ((rows, 2 * units), f32),
        ((n_ctx, rows, units), bf16),
        ((n_ctx, lines, wide), bf16),
        ((n_ctx, lines, wide), bf16),
        ((chunks * tokens, lines), bf16),
        ((heads // 2, 2 * tokens, n_ctx * tokens), bf16),
        ((heads // 2, 2 * tokens, HD), f32),
        ((order, order), bf16),
        ((order, order), bf16),
    ]
    need = sum(math.prod(s) * jnp.dtype(t).itemsize for s, t in scratch)
    hbm = pl.BlockSpec(memory_space=pltpu.HBM)
    vmem = pl.BlockSpec(memory_space=pltpu.VMEM)
    operands = (
        queries, key_rows, value_rows, stream, norm_gain.reshape(1, width),
        expert_ids.swapaxes(1, 2), gate_values.swapaxes(1, 2), w_gate, w_up, w_down,
    )
    return pl.pallas_call(
        functools.partial(fused, n_ctx, n_dp, (4, 6)),
        out_shape=(
            jax.ShapeDtypeStruct(queries.shape, bf16),
            jax.ShapeDtypeStruct(stream.shape, bf16),
        ),
        in_specs=[hbm] * 10,
        out_specs=(vmem, vmem),
        scratch_shapes=[pltpu.VMEM(s, t) for s, t in scratch]
        + [pltpu.SemaphoreType.DMA((n_ctx,))] * 12
        + [pltpu.SemaphoreType.DMA((10,))],
        compiler_params=pltpu.CompilerParams(
            collective_id=0, has_side_effects=True, vmem_limit_bytes=need + (16 << 20)
        ),
    )(*(pltpu.with_memory_space_constraint(x, pltpu.HBM) for x in operands))


def solution(mesh):
    rows = P("dp", "ctx", None)
    return jax.shard_map(
        functools.partial(shards, mesh.shape["ctx"], mesh.shape["dp"]),
        mesh=mesh,
        in_specs=(rows,) * 4 + (P(),) + (rows,) * 4 + (P("dp", None, "ctx"),),
        out_specs=(rows, rows),
        check_vma=False,
    )
```

profile of v0, /device:TPU:0, one launch (start us, length us, event | category | flops | bytes accessed | tf_op | source)
XLA Modules:
  0.0 44.1 jit_solution(4928328383613541292)
XLA Ops:
  0.6 41.9 %shard_map.113 = (bf16[1,128,2048]{2,1,0:T(8,128)(2,1)S(1)}, bf16[1,128,2048]{2,1,0:T(8,128)(2,1)S(1)}) custom-call(bf16[1,128,2048]{2,1,0:T(8,128)(2,1)} %q_hbm.1, bf16[1,128,256]{2,1,0:T(8,128)(2,1)} %k_hbm.1, bf16[1,128,256]{2,1,0:T(8,128)(2,1)} %v_hbm.1, bf16[1,128,2048]{2,1,0:T(8,128)(2,1)} %s_hbm.1, f32[1,2048]{1,0:T(1,128)} %bitcast.3, ...), custom_call_target="tpu_custom_call" | custom-call | tf_op jit(solution)/shard_map/pallas_call | solution.py:357
  42.5 0.8 %copy.14 = bf16[1,128,2048]{2,1,0:T(8,128)(2,1)} copy(bf16[1,128,2048]{2,1,0:T(8,128)(2,1)S(1)} %get-tuple-element.4) | data formatting | bytes 1048576
  43.3 0.8 %copy.15 = bf16[1,128,2048]{2,1,0:T(8,128)(2,1)} copy(bf16[1,128,2048]{2,1,0:T(8,128)(2,1)S(1)} %get-tuple-element.5) | data formatting | bytes 1048576
where the time goes:
time: 44.2 us; the launch traced here: 44.1 us
  Pallas kernels  41.9 us (95%)
  local copies, waits for them, and re-layouts  1.59 us (4%)
  between operations  0.64 us (1%)
    pallas_call x1, Pallas kernels, shards(): pl.pallas_call(functools.partial(fused, n_ctx, n_dp, (4, 6)), out_shape=(...  41.9 us
    unnamed x2, local copies, waits for them, and re-layouts  1.59 us

commit v1 on v0

--- a/solution.py
+++ b/solution.py
@@ -29,7 +29,7 @@
     att_ref, out_ref,
     q_ref, s_ref, normed_ref, gain_ref, ids_ref, gv_ref, wgu, wd_ref,
     outgoing, arrived, kbuf, vbuf, rs_out, rs_in, own, hid, answers, ret,
-    w_back, probs_ref, mass_ref, sort, unsort,
+    w_back, bias_ref, probs_ref, mass_ref, sort, unsort,
     k_send, k_recv, v_send, v_recv, a_send, a_recv, p_send, p_recv, h_send, h_recv,
     r_send, r_recv, load_sem,
 ):
@@ -76,26 +76,32 @@
 
     lax.fori_loop(1, total, greet, 0)
 
-    def parts_of(line):
-        rest = lax.rem(line, message)
-        return lax.div(line, message), lax.div(rest, slot), lax.rem(rest, slot)
-
-    expert, chunk, place_rank = parts_of(lax.broadcasted_iota(jnp.int32, (lines, 1), 0))
-    _, chunk_lane, rank_lane = parts_of(lax.broadcasted_iota(jnp.int32, (1, lines), 1))
-    expert_lane = lax.div(lax.broadcasted_iota(jnp.int32, (1, lines), 1), message)
+    def whole_part(number, size):
+        return jnp.floor((number + 0.5) * (1.0 / size))
+
+    def parts_of(shape, dim):
+        line = lax.broadcasted_iota(jnp.int32, shape, dim).astype(jnp.float32)
+        owner = whole_part(line, message)
+        rest = line - owner * message
+        piece = whole_part(rest, slot)
+        return owner, piece, rest - piece * slot
+
+    expert, chunk, place_rank = parts_of((lines, 1), 0)
+    expert_lane, chunk_lane, rank_lane = parts_of((1, lines), 1)
+    expert_id = expert.astype(jnp.int32)
     loads[0].wait()
     loads[1].wait()
     hot = jnp.zeros((lines, tokens), jnp.float32)
     weight = jnp.zeros((lines, tokens), jnp.float32)
     for t in range(ids_ref.shape[0]):
-        hit = ids_ref[t : t + 1, :] == expert
+        hit = ids_ref[t : t + 1, :] == expert_id
         hot = jnp.where(hit, 1.0, hot)
         weight = jnp.where(hit, gv_ref[t : t + 1, :], weight)
     rows_i = lax.broadcasted_iota(jnp.int32, (tokens, tokens), 0)
     cols_i = lax.broadcasted_iota(jnp.int32, (tokens, tokens), 1)
     before = jnp.where(rows_i < cols_i, 1.0, 0.0).astype(jnp.bfloat16)
     rank = jnp.dot(hot.astype(jnp.bfloat16), before, preferred_element_type=jnp.float32)
-    place = jnp.where(rank == place_rank.astype(jnp.float32), hot, 0.0)
+    place = jnp.where(rank == place_rank, hot, 0.0)
     select = jnp.concatenate(
         [jnp.where(chunk == j, place, 0.0).astype(jnp.bfloat16) for j in range(chunks)], axis=1
     )
@@ -124,7 +130,7 @@
             ).start()
             return carry
 
-        lax.fori_loop(first, n_dp, one, 0)
+        lax.fori_loop(first, n_dp, one, 0, unroll=n_dp <= 8)
 
     def group_of(buf, send, recv, c, rows):
         part = buf.at[c, pl.ds(0, rows)]
@@ -158,8 +164,8 @@
     arrived[my_c, my_rows] = outgoing[my_c, my_rows]
 
     if chunks > 1:
-        goes = chunk * rows_all + expert * slot + place_rank
-        goes_lane = chunk_lane * rows_all + expert_lane * slot + rank_lane
+        goes = (chunk * rows_all + expert * slot + place_rank).astype(jnp.int32)
+        goes_lane = (chunk_lane * rows_all + expert_lane * slot + rank_lane).astype(jnp.int32)
         square = (lines, lines)
         unsort[...] = jnp.where(
             lax.broadcasted_iota(jnp.int32, square, 1) == goes, 1.0, 0.0
@@ -175,7 +181,10 @@
         )
 
     keys = n_ctx * tokens
-    scale = 1.0 / math.sqrt(HD)
+    scale = math.log2(math.e) / math.sqrt(HD)
+    q_pos = my_c * tokens + lax.broadcasted_iota(jnp.int32, (tokens, keys), 0)
+    k_pos = lax.broadcasted_iota(jnp.int32, (tokens, keys), 1)
+    bias_ref[...] = jnp.where(k_pos <= q_pos, 0.0, hidden_score)
 
     def kv_lanes(pair):
         return pl.ds(pl.multiple_of((2 * pair // group) * HD, HD), HD)
@@ -190,11 +199,9 @@
                 two, kbuf[:, :, kv_lanes(pair)].reshape(keys, HD), (((1,), (1,)), ((), ())),
                 preferred_element_type=jnp.float32,
             ) * scale
-            q_pos = lax.broadcasted_iota(jnp.int32, (2 * tokens, keys), 0)
-            q_pos = my_c * tokens + jnp.where(q_pos < tokens, q_pos, q_pos - tokens)
-            k_pos = lax.broadcasted_iota(jnp.int32, (2 * tokens, keys), 1)
-            scores = jnp.where(k_pos <= q_pos, scores, hidden_score)
-            probs = jnp.exp(scores - jnp.max(scores, axis=-1, keepdims=True))
+            bias = bias_ref[...]
+            scores = scores + jnp.concatenate([bias, bias], axis=0)
+            probs = jnp.exp2(scores - jnp.max(scores, axis=-1, keepdims=True))
             mass = jnp.sum(probs, axis=-1, keepdims=True)
             probs_ref[pair] = probs.astype(jnp.bfloat16)
             mass_ref[pair] = jnp.broadcast_to(mass, (2 * tokens, HD))
@@ -202,18 +209,22 @@
 
         lax.fori_loop(first, last, one, 0)
 
+    def mix_pair(pair):
+        mixed = jnp.dot(
+            probs_ref[pair], vbuf[:, :, kv_lanes(pair)].reshape(keys, HD),
+            preferred_element_type=jnp.float32,
+        )
+        done = (mixed / mass_ref[pair]).astype(jnp.bfloat16)
+        for i in range(2):
+            att_ref[0, :, head_lanes(2 * pair + i)] = done[i * tokens : (i + 1) * tokens]
+
     def mix_values():
-        def one(pair, carry):
-            mixed = jnp.dot(
-                probs_ref[pair], vbuf[:, :, kv_lanes(pair)].reshape(keys, HD),
-                preferred_element_type=jnp.float32,
-            )
-            done = (mixed / mass_ref[pair]).astype(jnp.bfloat16)
-            for i in range(2):
-                att_ref[0, :, head_lanes(2 * pair + i)] = done[i * tokens : (i + 1) * tokens]
+        def one(step, carry):
+            mix_pair(2 * step)
+            mix_pair(2 * step + 1)
             return carry
 
-        lax.fori_loop(0, heads // 2, one, 0)
+        lax.fori_loop(0, heads // 4, one, 0)
 
     marks = [heads // 2 * part // 8 for part in split]
     loads[6].wait()
@@ -304,6 +315,17 @@
         ctx_copy(rs_out.at[c], rs_in.at[c], p_send.at[c], p_recv.at[c], c).wait_send()
         ctx_copy(hid.at[my_c], hid.at[c], h_send.at[c], h_recv.at[c], c).wait_send()
         group_of(answers, r_send, r_recv, c, lines).wait_send()
+
+
+def write_out(att_ref, out_ref, att_hbm, out_hbm, sems):
+    copies = [
+        pltpu.make_async_copy(att_ref, att_hbm, sems.at[0]),
+        pltpu.make_async_copy(out_ref, out_hbm, sems.at[1]),
+    ]
+    for copy in copies:
+        copy.start()
+    for copy in copies:
+        copy.wait()
 
 
 def shards(
@@ -342,6 +364,7 @@
         ((n_ctx, lines, wide), bf16),
         ((n_ctx, lines, wide), bf16),
         ((chunks * tokens, lines), bf16),
+        ((tokens, n_ctx * tokens), f32),
         ((heads // 2, 2 * tokens, n_ctx * tokens), bf16),
         ((heads // 2, 2 * tokens, HD), f32),
         ((order, order), bf16),
@@ -354,7 +377,7 @@
         queries, key_rows, value_rows, stream, norm_gain.reshape(1, width),
         expert_ids.swapaxes(1, 2), gate_values.swapaxes(1, 2), w_gate, w_up, w_down,
     )
-    return pl.pallas_call(
+    results = pl.pallas_call(
         functools.partial(fused, n_ctx, n_dp, (4, 6)),
         out_shape=(
             jax.ShapeDtypeStruct(queries.shape, bf16),
@@ -369,6 +392,14 @@
             collective_id=0, has_side_effects=True, vmem_limit_bytes=need + (16 << 20)
         ),
     )(*(pltpu.with_memory_space_constraint(x, pltpu.HBM) for x in operands))
+    return pl.pallas_call(
+        write_out,
+        out_shape=tuple(jax.ShapeDtypeStruct(r.shape, r.dtype) for r in results),
+        in_specs=[vmem, vmem],
+        out_specs=(hbm, hbm),
+        scratch_shapes=[pltpu.SemaphoreType.DMA((2,))],
+        compiler_params=pltpu.CompilerParams(vmem_limit_bytes=8 << 20),
+    )(*results)
 
 
 def solution(mesh):

time: 44.2 us -> 43.2 us (0.977)
  local copies, waits for them, and re-layouts: 1.59 us -> 0 us
  Pallas kernels: 41.9 us -> 42.4 us
    unnamed x2 -> x0, local copies, waits for them, and re-layouts: 1.59 us -> none
    pallas_call x0 -> x1, Pallas kernels: none -> 0.99 us  [shards(): pl.pallas_call(write_out, out_shape=tuple((jax.ShapeDtypeStruct(r.shape,...]
    pallas_call x1, Pallas kernels: 41.9 us -> 41.4 us  [shards(): pl.pallas_call(functools.partial(fused, n_ctx, n_dp, (4, 6)), out_shape=(...]
where the time goes in v1:
time: 43.2 us; the launch traced here: 43 us
  Pallas kernels  42.4 us (98%)
  between operations  0.64 us (1%)
    pallas_call x1, Pallas kernels, shards(): pl.pallas_call(functools.partial(fused, n_ctx, n_dp, (4, 6)), out_shape=(...  41.4 us
    pallas_call x1, Pallas kernels, shards(): pl.pallas_call(write_out, out_shape=tuple((jax.ShapeDtypeStruct(r.shape,...  0.99 us

profile of v1, /device:TPU:0, one launch (start us, length us, event | category | flops | bytes accessed | tf_op | source)
XLA Modules:
  0.0 43.0 jit_solution(11939315872217191925)
XLA Ops:
  0.6 41.4 %shard_map.113 = (bf16[1,128,2048]{2,1,0:T(8,128)(2,1)S(1)}, bf16[1,128,2048]{2,1,0:T(8,128)(2,1)S(1)}) custom-call(bf16[1,128,2048]{2,1,0:T(8,128)(2,1)} %q_hbm.1, bf16[1,128,256]{2,1,0:T(8,128)(2,1)} %k_hbm.1, bf16[1,128,256]{2,1,0:T(8,128)(2,1)} %v_hbm.1, bf16[1,128,2048]{2,1,0:T(8,128)(2,1)} %s_hbm.1, f32[1,2048]{1,0:T(1,128)} %bitcast.3, ...), custom_call_target="tpu_custom_call" | custom-call | tf_op jit(solution)/shard_map/pallas_call | solution.py:380
  42.1 1.0 %shard_map.114 = (bf16[1,128,2048]{2,1,0:T(8,128)(2,1)}, bf16[1,128,2048]{2,1,0:T(8,128)(2,1)}) custom-call(bf16[1,128,2048]{2,1,0:T(8,128)(2,1)S(1)} %get-tuple-element.4.att_ref, bf16[1,128,2048]{2,1,0:T(8,128)(2,1)S(1)} %get-tuple-element.5.out_ref), custom_call_target="tpu_custom_call" | custom-call | tf_op jit(solution)/shard_map/pallas_call | solution.py:395

commit v2 on v1

--- a/solution.py
+++ b/solution.py
@@ -76,6 +76,13 @@
 
     lax.fori_loop(1, total, greet, 0)
 
+    for c in range(1, n_ctx):
+
+        @pl.when(c > my_c)
+        def _(c=c):
+            kbuf[c] = jnp.zeros_like(kbuf[c])
+            vbuf[c] = jnp.zeros_like(vbuf[c])
+
     def whole_part(number, size):
         return jnp.floor((number + 0.5) * (1.0 / size))
 
@@ -117,9 +124,17 @@
     others = [lax.rem(my_c + i, n_ctx) for i in range(1, n_ctx)]
     my_rows = pl.ds(pl.multiple_of(my_d * message, message), message)
 
-    def scatter(src, dst, send, recv, c, first):
+    half = n_dp // 2
+    side = my_d // half
+
+    def nth_peer(i):
+        far = jnp.int32(i < half)
+        step = lax.rem(my_d + i + 1 - far, half)
+        return lax.rem(side + far, 2) * half + step
+
+    def scatter(src, dst, send, recv, c, last):
         def one(i, carry):
-            d = lax.rem(my_d + i, n_dp)
+            d = nth_peer(i)
             pltpu.make_async_remote_copy(
                 src_ref=src.at[c, pl.ds(pl.multiple_of(d * message, message), message)],
                 dst_ref=dst.at[my_c, my_rows],
@@ -130,7 +145,7 @@
             ).start()
             return carry
 
-        lax.fori_loop(first, n_dp, one, 0, unroll=n_dp <= 8)
+        lax.fori_loop(0, last, one, 0, unroll=n_dp <= 8)
 
     def group_of(buf, send, recv, c, rows):
         part = buf.at[c, pl.ds(0, rows)]
@@ -140,7 +155,11 @@
         )
 
     for c in others:
-        ctx_copy(k_hbm.at[0], kbuf.at[my_c], k_send.at[c], k_recv.at[my_c], c).start()
+
+        @pl.when(c > my_c)
+        def _(c=c):
+            ctx_copy(k_hbm.at[0], kbuf.at[my_c], k_send.at[c], k_recv.at[my_c], c).start()
+
 
     loads[2].wait()
     loads[3].wait()
@@ -160,7 +179,7 @@
         outgoing[c] = jnp.dot(select, stacked, preferred_element_type=jnp.float32).astype(
             jnp.bfloat16
         )
-        scatter(outgoing, arrived, a_send, a_recv, c, 1 if i == n_ctx - 1 else 0)
+        scatter(outgoing, arrived, a_send, a_recv, c, n_dp - 1 if i == n_ctx - 1 else n_dp)
     arrived[my_c, my_rows] = outgoing[my_c, my_rows]
 
     if chunks > 1:
@@ -230,7 +249,11 @@
     loads[6].wait()
     loads[8].wait()
     for c in others:
-        ctx_copy(k_hbm.at[0], kbuf.at[c], k_send.at[c], k_recv.at[c], c).wait_recv()
+
+        @pl.when(c < my_c)
+        def _(c=c):
+            ctx_copy(k_hbm.at[0], kbuf.at[c], k_send.at[c], k_recv.at[c], c).wait_recv()
+
     weigh(0, marks[0])
 
     def partial(c):
@@ -265,7 +288,11 @@
     for c in others:
         ctx_copy(hid.at[my_c], hid.at[my_c], h_send.at[c], h_recv.at[my_c], c).start()
     for c in others:
-        ctx_copy(v_hbm.at[0], vbuf.at[my_c], v_send.at[c], v_recv.at[my_c], c).start()
+
+        @pl.when(c > my_c)
+        def _(c=c):
+            ctx_copy(v_hbm.at[0], vbuf.at[my_c], v_send.at[c], v_recv.at[my_c], c).start()
+
 
     def answer(c):
         block = jnp.dot(hid[c], wd_ref[...], preferred_element_type=jnp.float32).astype(
@@ -281,15 +308,19 @@
         answers[c] = block
 
     answer(my_c)
-    scatter(answers, ret, r_send, r_recv, my_c, 1)
+    scatter(answers, ret, r_send, r_recv, my_c, n_dp - 1)
     ret[my_c, my_rows] = answers[my_c, my_rows]
     weigh(marks[1], heads // 2)
     for c in others:
         ctx_copy(hid.at[my_c], hid.at[c], h_send.at[c], h_recv.at[c], c).wait_recv()
         answer(c)
-        scatter(answers, ret, r_send, r_recv, c, 0)
-    for c in others:
-        ctx_copy(v_hbm.at[0], vbuf.at[c], v_send.at[c], v_recv.at[c], c).wait_recv()
+        scatter(answers, ret, r_send, r_recv, c, n_dp)
+    for c in others:
+
+        @pl.when(c < my_c)
+        def _(c=c):
+            ctx_copy(v_hbm.at[0], vbuf.at[c], v_send.at[c], v_recv.at[c], c).wait_recv()
+
     mix_values()
 
     def combine(c):
@@ -309,8 +340,12 @@
     group_of(outgoing, a_send, a_recv, my_c, lines - message).wait_send()
     group_of(answers, r_send, r_recv, my_c, lines - message).wait_send()
     for c in others:
-        ctx_copy(k_hbm.at[0], kbuf.at[c], k_send.at[c], k_recv.at[c], c).wait_send()
-        ctx_copy(v_hbm.at[0], vbuf.at[c], v_send.at[c], v_recv.at[c], c).wait_send()
+
+        @pl.when(c > my_c)
+        def _(c=c):
+            ctx_copy(k_hbm.at[0], kbuf.at[c], k_send.at[c], k_recv.at[c], c).wait_send()
+            ctx_copy(v_hbm.at[0], vbuf.at[c], v_send.at[c], v_recv.at[c], c).wait_send()
+
         group_of(outgoing, a_send, a_recv, c, lines).wait_send()
         ctx_copy(rs_out.at[c], rs_in.at[c], p_send.at[c], p_recv.at[c], c).wait_send()
         ctx_copy(hid.at[my_c], hid.at[c], h_send.at[c], h_recv.at[c], c).wait_send()

time: 43.2 us -> 42.7 us (0.988)
  Pallas kernels: 42.4 us -> 41.9 us
    pallas_call x1, Pallas kernels: 41.4 us -> 40.9 us  [shards(): pl.pallas_call(functools.partial(fused, n_ctx, n_dp, (4, 6)), out_shape=(...]
where the time goes in v2:
time: 42.7 us; the launch traced here: 42.6 us
  Pallas kernels  41.9 us (98%)
  between operations  0.64 us (1%)
    pallas_call x1, Pallas kernels, shards(): pl.pallas_call(functools.partial(fused, n_ctx, n_dp, (4, 6)), out_shape=(...  40.9 us
    pallas_call x1, Pallas kernels, shards(): pl.pallas_call(write_out, out_shape=tuple((jax.ShapeDtypeStruct(r.shape,...  0.99 us

profile of v2, /device:TPU:0, one launch (start us, length us, event | category | flops | bytes accessed | tf_op | source)
XLA Modules:
  0.0 42.6 jit_solution(9985904961312293632)
XLA Ops:
  0.6 40.9 %shard_map.113 = (bf16[1,128,2048]{2,1,0:T(8,128)(2,1)S(1)}, bf16[1,128,2048]{2,1,0:T(8,128)(2,1)S(1)}) custom-call(bf16[1,128,2048]{2,1,0:T(8,128)(2,1)} %q_hbm.1, bf16[1,128,256]{2,1,0:T(8,128)(2,1)} %k_hbm.1, bf16[1,128,256]{2,1,0:T(8,128)(2,1)} %v_hbm.1, bf16[1,128,2048]{2,1,0:T(8,128)(2,1)} %s_hbm.1, f32[1,2048]{1,0:T(1,128)} %bitcast.3, ...), custom_call_target="tpu_custom_call" | custom-call | tf_op jit(solution)/shard_map/pallas_call | solution.py:415
  41.6 1.0 %shard_map.114 = (bf16[1,128,2048]{2,1,0:T(8,128)(2,1)}, bf16[1,128,2048]{2,1,0:T(8,128)(2,1)}) custom-call(bf16[1,128,2048]{2,1,0:T(8,128)(2,1)S(1)} %get-tuple-element.4.att_ref, bf16[1,128,2048]{2,1,0:T(8,128)(2,1)S(1)} %get-tuple-element.5.out_ref), custom_call_target="tpu_custom_call" | custom-call | tf_op jit(solution)/shard_map/pallas_call | solution.py:430

commit v3 on v2

--- a/solution.py
+++ b/solution.py
@@ -24,7 +24,7 @@
 
 
 def fused(
-    n_ctx, n_dp, split,
+    n_ctx, n_dp,
     q_hbm, k_hbm, v_hbm, s_hbm, gain_hbm, ids_hbm, gv_hbm, wg_hbm, wu_hbm, wd_hbm,
     att_ref, out_ref,
     q_ref, s_ref, normed_ref, gain_ref, ids_ref, gv_ref, wgu, wd_ref,
@@ -245,7 +245,7 @@
 
         lax.fori_loop(0, heads // 4, one, 0)
 
-    marks = [heads // 2 * part // 8 for part in split]
+    marks = [heads // 2 * i // n_ctx for i in range(n_ctx + 1)]
     loads[6].wait()
     loads[8].wait()
     for c in others:
@@ -254,7 +254,7 @@
         def _(c=c):
             ctx_copy(k_hbm.at[0], kbuf.at[c], k_send.at[c], k_recv.at[c], c).wait_recv()
 
-    weigh(0, marks[0])
+    weigh(0, marks[1])
 
     def partial(c):
         block = arrived[c]
@@ -269,15 +269,15 @@
 
     loads[4].wait()
     loads[5].wait()
-    for c in others:
+    for i, c in enumerate(others):
         group_of(arrived, a_send, a_recv, c, lines).wait_recv()
         rs_out[c] = partial(c).astype(jnp.bfloat16)
         ctx_copy(rs_out.at[c], rs_in.at[my_c], p_send.at[c], p_recv.at[my_c], c).start()
+        weigh(marks[i + 1], marks[i + 2])
     group_of(arrived, a_send, a_recv, my_c, lines - message).wait_recv()
     own[...] = partial(my_c)
     loads[7].wait()
     loads[9].wait()
-    weigh(marks[0], marks[1])
     for c in others:
         ctx_copy(rs_out.at[c], rs_in.at[c], p_send.at[c], p_recv.at[c], c).wait_recv()
     sums = own[...]
@@ -310,7 +310,6 @@
     answer(my_c)
     scatter(answers, ret, r_send, r_recv, my_c, n_dp - 1)
     ret[my_c, my_rows] = answers[my_c, my_rows]
-    weigh(marks[1], heads // 2)
     for c in others:
         ctx_copy(hid.at[my_c], hid.at[c], h_send.at[c], h_recv.at[c], c).wait_recv()
         answer(c)
@@ -413,7 +412,7 @@
         expert_ids.swapaxes(1, 2), gate_values.swapaxes(1, 2), w_gate, w_up, w_down,
     )
     results = pl.pallas_call(
-        functools.partial(fused, n_ctx, n_dp, (4, 6)),
+        functools.partial(fused, n_ctx, n_dp),
         out_shape=(
             jax.ShapeDtypeStruct(queries.shape, bf16),
             jax.ShapeDtypeStruct(stream.shape, bf16),

time: 42.7 us -> 44.3 us (1.037)
  Pallas kernels: 41.9 us -> 43.5 us
    pallas_call x1, Pallas kernels: 40.9 us -> 42.5 us  [shards(): pl.pallas_call(functools.partial(fused, n_ctx, n_dp), out_shape=(jax.Shap...]
where the time goes in v3:
time: 44.3 us; the launch traced here: 44.2 us
  Pallas kernels  43.5 us (98%)
  between operations  0.64 us (1%)
    pallas_call x1, Pallas kernels, shards(): pl.pallas_call(functools.partial(fused, n_ctx, n_dp), out_shape=(jax.Shap...  42.5 us
    pallas_call x1, Pallas kernels, shards(): pl.pallas_call(write_out, out_shape=tuple((jax.ShapeDtypeStruct(r.shape,...  0.99 us

profile of v3, /device:TPU:0, one launch (start us, length us, event | category | flops | bytes accessed | tf_op | source)
XLA Modules:
  0.0 44.2 jit_solution(16403434362929608165)
XLA Ops:
  0.6 42.5 %shard_map.113 = (bf16[1,128,2048]{2,1,0:T(8,128)(2,1)S(1)}, bf16[1,128,2048]{2,1,0:T(8,128)(2,1)S(1)}) custom-call(bf16[1,128,2048]{2,1,0:T(8,128)(2,1)} %q_hbm.1, bf16[1,128,256]{2,1,0:T(8,128)(2,1)} %k_hbm.1, bf16[1,128,256]{2,1,0:T(8,128)(2,1)} %v_hbm.1, bf16[1,128,2048]{2,1,0:T(8,128)(2,1)} %s_hbm.1, f32[1,2048]{1,0:T(1,128)} %bitcast.3, ...), custom_call_target="tpu_custom_call" | custom-call | tf_op jit(solution)/shard_map/pallas_call | solution.py:414
  43.2 1.0 %shard_map.114 = (bf16[1,128,2048]{2,1,0:T(8,128)(2,1)}, bf16[1,128,2048]{2,1,0:T(8,128)(2,1)}) custom-call(bf16[1,128,2048]{2,1,0:T(8,128)(2,1)S(1)} %get-tuple-element.4.att_ref, bf16[1,128,2048]{2,1,0:T(8,128)(2,1)S(1)} %get-tuple-element.5.out_ref), custom_call_target="tpu_custom_call" | custom-call | tf_op jit(solution)/shard_map/pallas_call | solution.py:429
